TPU v7x, 128 devices: a whole 4x4x4 slice. The times are simulated.
128 devices in a mesh: section: 2 (over x_lo), dp: 32 (over y, z, core), tensor: 2 (over x_hi).
Axes of the slice: x: 4 (x_hi: 2, x_lo: 2; x = x_hi * 2 + x_lo), y: 4, z: 4, core: 2. Of those that a mesh axis runs over, the one named last changes fastest.
Arguments:
- tokens_in: bfloat16 [2, 8192, 768], P(None, ('dp', 'tensor')), may hold values from -6 to 6
- cotangent: bfloat16 [2, 8192, 768], P(None, ('dp', 'tensor')), may hold values from -6 to 6
- place: int32 [32], replicated, may hold values from 0 to 31, each once
- w_qkv: bfloat16 [2, 3, 768, 768], P('section', None, 'dp', 'tensor'), may hold values from -0.21875 to 0.21875
- w_out: bfloat16 [2, 768, 768], P('section', 'tensor', 'dp'), may hold values from -1.75 to 1.75
- w_up: bfloat16 [2, 768, 3072], P('section', 'dp', 'tensor'), may hold values from -0.21875 to 0.21875
- w_down: bfloat16 [2, 3072, 768], P('section', 'tensor', 'dp'), may hold values from -0.109375 to 0.109375
- qv_bias: bfloat16 [2, 2, 768], P('section', None, 'tensor'), may hold values from -0.59765625 to 0.59765625
- up_bias: bfloat16 [2, 3072], P('section', 'tensor'), may hold values from -3 to 3
- vectors: bfloat16 [2, 6, 768], P('section'), may hold values from -1.5 to 2
Outputs:
- acts: bfloat16 [2, 2, 8192, 768], P('section', None, ('dp', 'tensor'))
- input_grads: float32 [2, 2, 8192, 768], P('section', None, ('dp', 'tensor'))
- grad_w_qkv: float32 [2, 3, 768, 768], P('section', None, 'dp', 'tensor')
- grad_w_out: float32 [2, 768, 768], P('section', 'tensor', 'dp')
- grad_w_up: float32 [2, 768, 3072], P('section', 'dp', 'tensor')
- grad_w_down: float32 [2, 3072, 768], P('section', 'tensor', 'dp')
- grad_qv_bias: float32 [2, 2, 768], P('section', None, 'tensor')
- grad_up_bias: float32 [2, 3072], P('section', 'tensor')
- grad_vectors: float32 [2, 6, 768], P('section')
Inputs may be any that keep to these rules, and one draw needn't show every extreme that they name: A permutation; block d of every micro-batch is part place[d] mod 8 of sequence place[d] div 8.
All inputs are finite; a program needn't handle non-finite values.
Results may differ from a plain program's by a relative error of at most 0.017.
Values may be sent and summed in bfloat16 or wider, within the bound.
A program may use at most 256 MiB of HBM per device.

v0:
```python
import jax
import jax.numpy as jnp
from jax import lax
from jax.sharding import PartitionSpec as P

HEAD_DIM = 64
PIECES = 8


epsilon = 1e-05
masked_value = -1e30


def passed_along(block, axis, distance):
    devices = range(lax.axis_size(axis))
    route = [(i - distance, i) for i in devices if i - distance in devices]
    return lax.ppermute(block, axis, route)


def normalize(residual, gain_row, shift_row):
    average = jnp.mean(residual, axis=-1, keepdims=True)
    centred = residual - average
    spread = jnp.mean(centred * centred, axis=-1, keepdims=True)
    return centred * lax.rsqrt(spread + epsilon) * gain_row + shift_row


def smooth_gate(values):
    return jax.nn.gelu(values, approximate=False)


def matmul(left, right):
    return jnp.dot(left, right, preferred_element_type=jnp.float32)


def inner_left(left, right):
    return lax.dot_general(
        left, right, (((0,), (0,)), ((), ())), preferred_element_type=jnp.float32
    )


def inner_right(left, right):
    return lax.dot_general(
        left, right, (((1,), (1,)), ((), ())), preferred_element_type=jnp.float32
    )


def gather_rows(values):
    return lax.all_gather(values, "tensor", axis=0, tiled=True)


def scatter_rows(values):
    return lax.psum_scatter(
        values.astype(jnp.bfloat16), "tensor", scatter_dimension=0, tiled=True
    ).astype(jnp.float32)


def gather_grads(values):
    return lax.all_gather(values, "tensor", axis=0, tiled=True)


def scatter_grads(values):
    return lax.psum_scatter(
        values.astype(jnp.bfloat16), "tensor", scatter_dimension=0, tiled=True
    ).astype(jnp.float32)


def soft_weights(query_heads, key_heads, query_place, key_place, log_total):
    scores = jnp.einsum("qhd,khd->hqk", query_heads, key_heads, preferred_element_type=jnp.float32)
    allowed = (query_place[:, None] >= key_place[None, :])[None]
    return jnp.where(allowed, jnp.exp(jnp.where(allowed, scores, masked_value) - log_total), 0.0)


def on_device(tokens_in, cotangent, place, w_qkv, w_out, w_up, w_down, qv_bias, up_bias, vectors):
    section_at = lax.axis_index("section")
    section_count = lax.axis_size("section")
    block_count = lax.axis_size("dp")
    micro_count = tokens_in.shape[0]
    tick_count = micro_count + section_count - 1
    block_rows = tokens_in.shape[1] * lax.axis_size("tensor")
    length = PIECES * block_rows
    score_scale = HEAD_DIM ** (-0.5)
    full_qkv, full_out, full_up, full_down = (
        lax.all_gather(w_qkv, "dp", axis=2, tiled=True),
        lax.all_gather(w_out, "dp", axis=2, tiled=True),
        lax.all_gather(w_up, "dp", axis=1, tiled=True),
        lax.all_gather(w_down, "dp", axis=2, tiled=True),
    )
    proj_qkv = full_qkv[0]
    proj_out = full_out[0]
    proj_up = full_up[0]
    proj_down = full_down[0]
    bias_qv = qv_bias[0].astype(jnp.float32)
    bias_up = up_bias[0].astype(jnp.float32)
    vector_rows = vectors[0].astype(jnp.float32)
    inverse = (
        jnp.zeros((block_count,), jnp.int32).at[place].set(jnp.arange(block_count, dtype=jnp.int32))
    )
    own_place = place[lax.axis_index("dp")]
    part_index = own_place % PIECES
    blocks = lax.dynamic_slice_in_dim(inverse, own_place - part_index, PIECES)
    query_place = part_index * block_rows + jnp.arange(block_rows)
    key_place = jnp.arange(length)

    def select_blocks(whole):
        return whole.reshape((block_count, block_rows) + whole.shape[1:])[blocks].reshape(
            (length,) + whole.shape[1:]
        )

    received = jnp.zeros(tokens_in.shape[1:], jnp.bfloat16)
    outputs = []
    states = []
    for moment in range(tick_count):
        own_rows = tokens_in[min(moment, micro_count - 1)]
        entering = jnp.where(section_at == 0, own_rows, received).astype(jnp.float32)
        forward_normed = gather_rows(
            normalize(entering, vector_rows[0], vector_rows[1]).astype(jnp.bfloat16)
        )
        forward_query_rows = (
            (matmul(forward_normed, proj_qkv[0]) + bias_qv[0]) * score_scale
        ).astype(jnp.bfloat16)
        forward_key_rows = matmul(forward_normed, proj_qkv[1]).astype(jnp.bfloat16)
        forward_value_rows = (matmul(forward_normed, proj_qkv[2]) + bias_qv[1]).astype(jnp.bfloat16)
        key_all = lax.all_gather(forward_key_rows, "dp", axis=0, tiled=True)
        value_all = lax.all_gather(forward_value_rows, "dp", axis=0, tiled=True)
        forward_key_heads = select_blocks(key_all).reshape(length, -1, HEAD_DIM)
        forward_value_heads = select_blocks(value_all).reshape(length, -1, HEAD_DIM)
        forward_query_heads = forward_query_rows.reshape(block_rows, -1, HEAD_DIM)
        scores = jnp.einsum(
            "qhd,khd->hqk",
            forward_query_heads,
            forward_key_heads,
            preferred_element_type=jnp.float32,
        )
        allowed = (query_place[:, None] >= key_place[None, :])[None]
        scores = jnp.where(allowed, scores, masked_value)
        largest = jnp.max(scores, axis=-1, keepdims=True)
        forward_log_total = largest + jnp.log(
            jnp.sum(jnp.exp(scores - largest), axis=-1, keepdims=True)
        )
        forward_attention = jnp.where(allowed, jnp.exp(scores - forward_log_total), 0.0)
        forward_mixed_heads = jnp.einsum(
            "hqk,khd->qhd",
            forward_attention.astype(jnp.bfloat16),
            forward_value_heads,
            preferred_element_type=jnp.float32,
        )
        forward_mixed_heads = forward_mixed_heads.reshape(block_rows, -1).astype(jnp.bfloat16)
        forward_hidden = (
            entering + scatter_rows(matmul(forward_mixed_heads, proj_out)) + vector_rows[2]
        )
        forward_normed_two = gather_rows(
            normalize(forward_hidden, vector_rows[3], vector_rows[4]).astype(jnp.bfloat16)
        )
        forward_pre_active = matmul(forward_normed_two, proj_up) + bias_up
        forward_active = smooth_gate(forward_pre_active).astype(jnp.bfloat16)
        leaving = forward_hidden + scatter_rows(matmul(forward_active, proj_down)) + vector_rows[5]
        forward_kept_state = (
            entering,
            forward_normed,
            forward_query_rows,
            forward_key_rows,
            forward_value_rows,
            forward_key_heads,
            forward_value_heads,
            forward_log_total,
            forward_mixed_heads,
            forward_hidden,
            forward_normed_two,
            forward_pre_active,
            forward_active,
        )
        leaving, kept_state = (leaving, forward_kept_state)
        low_out = leaving.astype(jnp.bfloat16)
        outputs.append(low_out)
        states.append(kept_state)
        if moment + 1 < tick_count:
            received = passed_along(low_out, "section", 1)
    stacked_states = jax.tree.map(lambda *parts: jnp.stack(parts), *states)
    stacked_out = jnp.stack(outputs)
    incoming = jnp.zeros(cotangent.shape[1:], jnp.bfloat16)
    accrued = None
    input_list = []
    for moment in range(tick_count):
        if moment < micro_count:
            own_grad = cotangent[moment]
        else:
            own_grad = jnp.zeros(cotangent.shape[1:], jnp.bfloat16)
        arriving = jnp.where(section_at == section_count - 1, own_grad, incoming)
        slot_index = jnp.clip(moment - section_count + 1 + 2 * section_at, 0, tick_count - 1)
        kept_state = jax.tree.map(
            lambda stacked: lax.dynamic_index_in_dim(stacked, slot_index, 0, False), stacked_states
        )
        (
            residual,
            normed,
            query_rows,
            key_rows,
            value_rows,
            key_heads,
            value_heads,
            log_total,
            mixed_heads,
            hidden,
            normed_two,
            pre_active,
            active,
        ) = kept_state
        carried = arriving.astype(jnp.float32)
        grad_down_bias = jnp.sum(carried, axis=0)
        carried_all = gather_grads(arriving)
        backward_grad_down = inner_left(active, carried_all)
        grad_active = inner_right(carried_all, proj_down)
        gate_back = jax.vjp(smooth_gate, pre_active)[1]
        grad_pre = gate_back(grad_active)[0].astype(jnp.bfloat16)
        backward_grad_up_bias = jnp.sum(grad_pre.astype(jnp.float32), axis=0)
        backward_grad_up = inner_left(normed_two, grad_pre)
        grad_normed_two = scatter_grads(inner_right(grad_pre, proj_up))
        norm_back_two = jax.vjp(normalize, hidden, vector_rows[3], vector_rows[4])[1]
        through_two, grad_gain_two, grad_shift_two = norm_back_two(grad_normed_two)
        grad_hidden = carried + through_two
        grad_hidden_low = grad_hidden.astype(jnp.bfloat16)
        grad_out_bias = jnp.sum(grad_hidden_low.astype(jnp.float32), axis=0)
        hidden_all = gather_grads(grad_hidden_low)
        backward_grad_out = inner_left(mixed_heads, hidden_all)
        grad_mixed = inner_right(hidden_all, proj_out).astype(jnp.bfloat16)
        grad_heads = grad_mixed.reshape(block_rows, -1, HEAD_DIM)
        query_heads = query_rows.reshape(block_rows, -1, HEAD_DIM)
        attention = soft_weights(query_heads, key_heads, query_place, key_place, log_total)
        grad_soft = jnp.einsum(
            "qhd,khd->hqk", grad_heads, value_heads, preferred_element_type=jnp.float32
        )
        row_dots = jnp.sum(attention * grad_soft, axis=-1, keepdims=True)
        grad_scores = (attention * (grad_soft - row_dots)).astype(jnp.bfloat16)
        grad_query = jnp.einsum(
            "hqk,khd->qhd", grad_scores, key_heads, preferred_element_type=jnp.float32
        )
        grad_query = grad_query.reshape(block_rows, -1).astype(jnp.bfloat16)
        grad_query = (grad_query.astype(jnp.float32) * score_scale).astype(jnp.bfloat16)
        query_all = lax.all_gather(query_rows, "dp", axis=0, tiled=True)
        grad_all = lax.all_gather(grad_mixed, "dp", axis=0, tiled=True)
        total_all = lax.all_gather(log_total[:, :, 0].T, "dp", axis=0, tiled=True)
        dots_all = lax.all_gather(row_dots[:, :, 0].T, "dp", axis=0, tiled=True)
        query_seq = select_blocks(query_all).reshape(length, -1, HEAD_DIM)
        grad_seq = select_blocks(grad_all).reshape(length, -1, HEAD_DIM)
        total_seq = select_blocks(total_all).T[:, :, None]
        dots_seq = select_blocks(dots_all).T[:, :, None]
        own_keys = key_rows.reshape(block_rows, -1, HEAD_DIM)
        own_values = value_rows.reshape(block_rows, -1, HEAD_DIM)
        side_weights = soft_weights(query_seq, own_keys, key_place, query_place, total_seq)
        side_soft = jnp.einsum(
            "qhd,khd->hqk", grad_seq, own_values, preferred_element_type=jnp.float32
        )
        side_scores = (side_weights * (side_soft - dots_seq)).astype(jnp.bfloat16)
        grad_key = jnp.einsum(
            "hqk,qhd->khd", side_scores, query_seq, preferred_element_type=jnp.float32
        ).reshape(block_rows, -1)
        grad_value = jnp.einsum(
            "hqk,qhd->khd",
            side_weights.astype(jnp.bfloat16),
            grad_seq,
            preferred_element_type=jnp.float32,
        ).reshape(block_rows, -1)
        grad_key = grad_key.astype(jnp.bfloat16)
        grad_value = grad_value.astype(jnp.bfloat16)
        backward_grad_qkv = jnp.stack(
            [
                inner_left(normed, grad_query),
                inner_left(normed, grad_key),
                inner_left(normed, grad_value),
            ]
        )
        backward_grad_qv = jnp.stack(
            [
                jnp.sum(grad_query.astype(jnp.float32), axis=0),
                jnp.sum(grad_value.astype(jnp.float32), axis=0),
            ]
        )
        grad_normed = (
            inner_right(grad_query, proj_qkv[0])
            + inner_right(grad_key, proj_qkv[1])
            + inner_right(grad_value, proj_qkv[2])
        )
        grad_normed_rows = scatter_grads(grad_normed)
        norm_back_one = jax.vjp(normalize, residual, vector_rows[0], vector_rows[1])[1]
        through_one, grad_gain_one, grad_shift_one = norm_back_one(grad_normed_rows)
        grad_input = grad_hidden + through_one
        backward_grad_vector = jnp.stack(
            [
                grad_gain_one,
                grad_shift_one,
                grad_out_bias,
                grad_gain_two,
                grad_shift_two,
                grad_down_bias,
            ]
        )
        grad_input, gradients = (
            grad_input,
            (
                backward_grad_qkv,
                backward_grad_out,
                backward_grad_up,
                backward_grad_down,
                backward_grad_qv,
                backward_grad_up_bias,
                backward_grad_vector,
            ),
        )
        accrued = gradients if accrued is None else jax.tree.map(jnp.add, accrued, gradients)
        input_list.append(grad_input)
        if moment + 1 < tick_count:
            incoming = passed_along(grad_input.astype(jnp.bfloat16), "section", -1)
    stacked_inputs = jnp.stack(input_list)
    acts = jnp.stack(
        [
            lax.dynamic_index_in_dim(stacked_out, micro_index + section_at, 0, False)
            for micro_index in range(micro_count)
        ]
    )[None]
    input_grads = jnp.stack(
        [
            lax.dynamic_index_in_dim(
                stacked_inputs, micro_index + section_count - 1 - section_at, 0, False
            )
            for micro_index in range(micro_count)
        ]
    )[None]
    grad_qkv, grad_out, grad_up, grad_down, grad_qv, grad_up_bias, grad_vector = accrued
    sum_qkv, sum_out, sum_up, sum_down = (
        lax.psum_scatter(
            grad_qkv[None].astype(jnp.bfloat16), "dp", scatter_dimension=2, tiled=True
        ).astype(jnp.float32),
        lax.psum_scatter(
            grad_out[None].astype(jnp.bfloat16), "dp", scatter_dimension=2, tiled=True
        ).astype(jnp.float32),
        lax.psum_scatter(
            grad_up[None].astype(jnp.bfloat16), "dp", scatter_dimension=1, tiled=True
        ).astype(jnp.float32),
        lax.psum_scatter(
            grad_down[None].astype(jnp.bfloat16), "dp", scatter_dimension=2, tiled=True
        ).astype(jnp.float32),
    )
    sum_qv, sum_up_bias = lax.psum((grad_qv[None], grad_up_bias[None]), "dp")
    sum_vector = lax.psum(grad_vector[None], ("dp", "tensor"))
    return (acts, input_grads, sum_qkv, sum_out, sum_up, sum_down, sum_qv, sum_up_bias, sum_vector)


def solution(mesh):
    placed = (
        P(None, ("dp", "tensor"), None),
        P(None, ("dp", "tensor"), None),
        P(),
        P("section", None, "dp", "tensor"),
        P("section", "tensor", "dp"),
        P("section", "dp", "tensor"),
        P("section", "tensor", "dp"),
        P("section", None, "tensor"),
        P("section", "tensor"),
        P("section", None, None),
    )
    return jax.shard_map(
        on_device,
        mesh=mesh,
        in_specs=placed,
        out_specs=(
            P("section", None, ("dp", "tensor"), None),
            P("section", None, ("dp", "tensor"), None),
            P("section", None, "dp", "tensor"),
            P("section", "tensor", "dp"),
            P("section", "dp", "tensor"),
            P("section", "tensor", "dp"),
            P("section", None, "tensor"),
            P("section", "tensor"),
            P("section", None, None),
        ),
        check_vma=False,
    )
```

profile of v0, /device:TPU:1, one launch (start us, length us, event | category | flops | bytes accessed | tf_op | source)
XLA Modules:
  0.0 1904.6 jit_solution(6889812153780601305)
XLA Ops:
  21.1 36.6 %all-gather.20.cloned.1.call-done = bf16[1,3,768,384]{3,2,1,0:T(8,128)(2,1)} async-done(((bf16[1,3,24,384]{3,2,1,0:T(8,128)(2,1)}), bf16[1,3,768,384]{3,2,1,0:T(8,128)(2,1)}) %all-gather.20.cloned.1.call-update) | async-done | bytes 1769488 | tf_op jit(solution)/shard_map/all_gather | solution.py:83
  66.2 24.3 %all_gather.106 = bf16[1,384,768]{1,2,0:T(8,128)(2,1)S(1)} all-gather(bf16[1,384,24]{1,2,0:T(8,128)(2,1)S(1)} %copy-done.119), channel_id=1, replica_groups=mesh['section'=2,'dp'=32,'tensor'=2] {'dp'}, dimensions={2}, use_global_device_ids=true | all-gather | bytes 608256 | tf_op jit(solution)/shard_map/all_gather | solution.py:84
  91.4 17.2 all-gather.22.cloned.1.call-done
  120.1 39.0 %all-gather.24.cloned.1.call-done = bf16[8192,384]{1,0:T(8,128)(2,1)} async-done(((bf16[256,384]{1,0:T(8,128)(2,1)}), bf16[8192,384]{1,0:T(8,128)(2,1)}) %all-gather.24.cloned.1.call-update) | async-done | bytes 6291472 | tf_op jit(solution)/shard_map/all_gather | solution.py:123
  210.0 34.5 %all-gather.26.cloned.1.call-done = bf16[1,768,1536]{2,1,0:T(8,128)(2,1)} async-done(((bf16[1,24,1536]{2,1,0:T(8,128)(2,1)}), bf16[1,768,1536]{2,1,0:T(8,128)(2,1)}) %all-gather.26.cloned.1.call-update) | async-done | bytes 2359312 | tf_op jit(solution)/shard_map/all_gather | solution.py:85
  251.5 39.0 %all-gather.28.cloned.1.call-done = bf16[1,1536,768]{1,2,0:T(8,128)(2,1)} async-done(((bf16[1,1536,24]{1,2,0:T(8,128)(2,1)}), bf16[1,1536,768]{1,2,0:T(8,128)(2,1)}) %all-gather.28.cloned.1.call-update) | async-done | bytes 2359312 | tf_op jit(solution)/shard_map/all_gather | solution.py:86
  294.1 16.1 reduce-scatter.17.cloned.1.call-done
  333.1 47.0 %all-gather.30.cloned.1.call-done = bf16[8192,384]{1,0:T(8,128)(2,1)} async-done(((bf16[256,384]{1,0:T(8,128)(2,1)}), bf16[8192,384]{1,0:T(8,128)(2,1)}) %all-gather.30.cloned.1.call-update) | async-done | bytes 6291472 | tf_op jit(solution)/shard_map/all_gather | solution.py:124
  391.6 39.0 %all-gather.32.cloned.1.call-done = bf16[8192,384]{1,0:T(8,128)(2,1)} async-done(((bf16[256,384]{1,0:T(8,128)(2,1)}), bf16[8192,384]{1,0:T(8,128)(2,1)}) %all-gather.32.cloned.1.call-update) | async-done | bytes 6291472 | tf_op jit(solution)/shard_map/all_gather | solution.py:123
  454.6 15.7 reduce-scatter.19.cloned.1.call-done
  489.7 17.5 reduce-scatter.21.cloned.1.call-done
  529.8 47.5 %all-gather.34.cloned.1.call-done = bf16[8192,384]{1,0:T(8,128)(2,1)} async-done(((bf16[256,384]{1,0:T(8,128)(2,1)}), bf16[8192,384]{1,0:T(8,128)(2,1)}) %all-gather.34.cloned.1.call-update) | async-done | bytes 6291472 | tf_op jit(solution)/shard_map/all_gather | solution.py:124
  586.7 41.1 %all-gather.36.cloned.1.call-done = bf16[8192,384]{1,0:T(8,128)(2,1)} async-done(((bf16[256,384]{1,0:T(8,128)(2,1)}), bf16[8192,384]{1,0:T(8,128)(2,1)}) %all-gather.36.cloned.1.call-update) | async-done | bytes 6291472 | tf_op jit(solution)/shard_map/all_gather | solution.py:123
  775.3 28.9 %all_gather.121 = f32[8192,6]{0,1:T(8,128)} all-gather(f32[256,6]{0,1:T(8,128)S(1)} %get-tuple-element.146), channel_id=1, replica_groups=mesh['section'=2,'dp'=32,'tensor'=2] {'dp'}, dimensions={0}, use_global_device_ids=true | all-gather | bytes 202752 | tf_op jit(solution)/shard_map/all_gather | solution.py:241
  837.2 25.9 %all_gather.123 = f32[8192,6]{0,1:T(8,128)} all-gather(f32[256,6]{0,1:T(8,128)S(1)} %bitcast.945), channel_id=1, replica_groups=mesh['section'=2,'dp'=32,'tensor'=2] {'dp'}, dimensions={0}, use_global_device_ids=true | all-gather | bytes 202752 | tf_op jit(solution)/shard_map/all_gather | solution.py:242
  960.2 17.2 reduce-scatter.31.cloned.1.call-done
  996.3 32.5 %all-gather.46.cloned.1.call-done = bf16[1,8192,384]{2,1,0:T(8,128)(2,1)} async-done(((bf16[1,256,384]{2,1,0:T(8,128)(2,1)}), bf16[1,8192,384]{2,1,0:T(8,128)(2,1)}) %all-gather.46.cloned.1.call-update) | async-done | bytes 6291472 | tf_op jit(solution)/shard_map/all_gather | solution.py:239
  1040.3 26.2 %all_gather.127 = f32[8192,6]{0,1:T(8,128)} all-gather(f32[256,6]{0,1:T(8,128)S(1)} %copy-done.116), channel_id=1, replica_groups=mesh['section'=2,'dp'=32,'tensor'=2] {'dp'}, dimensions={0}, use_global_device_ids=true | all-gather | bytes 202752 | tf_op jit(solution)/shard_map/all_gather | solution.py:241
  1095.5 25.2 %all_gather.129 = f32[8192,6]{0,1:T(8,128)} all-gather(f32[256,6]{0,1:T(8,128)S(1)} %bitcast.946), channel_id=1, replica_groups=mesh['section'=2,'dp'=32,'tensor'=2] {'dp'}, dimensions={0}, use_global_device_ids=true | all-gather | bytes 202752 | tf_op jit(solution)/shard_map/all_gather | solution.py:242
  1255.5 32.6 %all-gather.48.cloned.1.call-done = bf16[1,8192,384]{2,1,0:T(8,128)(2,1)} async-done(((bf16[1,256,384]{2,1,0:T(8,128)(2,1)}), bf16[1,8192,384]{2,1,0:T(8,128)(2,1)}) %all-gather.48.cloned.1.call-update) | async-done | bytes 6291472 | tf_op jit(solution)/shard_map/all_gather | solution.py:239
  1299.4 24.1 %all_gather.133 = f32[8192,6]{0,1:T(8,128)S(1)} all-gather(f32[256,6]{0,1:T(8,128)S(1)} %copy-done.115), channel_id=1, replica_groups=mesh['section'=2,'dp'=32,'tensor'=2] {'dp'}, dimensions={0}, use_global_device_ids=true | all-gather | bytes 202752 | tf_op jit(solution)/shard_map/all_gather | solution.py:241
  1420.2 23.0 %all_gather.135 = f32[8192,6]{0,1:T(8,128)S(1)} all-gather(f32[256,6]{0,1:T(8,128)S(1)} %bitcast.944), channel_id=1, replica_groups=mesh['section'=2,'dp'=32,'tensor'=2] {'dp'}, dimensions={0}, use_global_device_ids=true | all-gather | bytes 202752 | tf_op jit(solution)/shard_map/all_gather | solution.py:242
  1496.1 65.7 %all-reduce.3 = (f32[1,2,384]{2,1,0:T(2,128)}, f32[1,1536]{1,0:T(1,128)}) all-reduce(f32[1,2,384]{2,1,0:T(2,128)S(1)} %fusion.411, f32[1,1536]{1,0:T(1,128)S(1)} %add.730), channel_id=1, replica_groups=mesh['section'=2,'dp'=32,'tensor'=2] {'dp'}, use_global_device_ids=true, to_apply=%region_68.69 | all-reduce | flops 2304 | bytes 18432 | tf_op jit(solution)/shard_map/psum | solution.py:343
  1564.3 326.5 %psum.23 = f32[1,6,768]{2,0,1:T(1,128)} all-reduce(f32[1,6,768]{2,0,1:T(1,128)S(1)} %add_add_fusion.8), channel_id=1, replica_groups=mesh['section'=2,'dp'=32,'tensor'=2] {'dp','tensor'}, use_global_device_ids=true, to_apply=%region_91.92 | all-reduce | flops 4608 | bytes 36864 | tf_op jit(solution)/shard_map/psum | solution.py:344
  (753 shorter events, 842.7 us)
Async XLA Ops:
  7.9 100.8 %all-gather.22.cloned.1.call-start = ((), (), s32[]{:S(2)}) async-start(), calls=%async_computation.14 | async-start | bytes 6488064 | tf_op jit(solution)/shard_map/all_gather | solution.py:124
  59.9 99.2 %all-gather.24.cloned.1.call-start = ((), (), s32[]{:S(2)}) async-start(), calls=%async_computation.15 | async-start | bytes 6488064 | tf_op jit(solution)/shard_map/all_gather | solution.py:123
  62.2 135.7 %reduce-scatter.15.cloned.1.call-start = ((), (), s32[]{:S(2)}) async-start(), calls=%async_computation.16 | async-start | bytes 589824 | tf_op jit(solution)/shard_map/reduce_scatter | solution.py:52
  182.8 107.7 %all-gather.28.cloned.1.call-start = ((), (), s32[]{:S(2)}) async-start(), calls=%async_computation.18 | async-start | bytes 2433024 | tf_op jit(solution)/shard_map/all_gather | solution.py:86
  183.3 126.8 %reduce-scatter.17.cloned.1.call-start = ((), (), s32[]{:S(2)}) async-start(), calls=%async_computation.19 | async-start | bytes 589824 | tf_op jit(solution)/shard_map/reduce_scatter | solution.py:52
  294.0 86.2 %all-gather.30.cloned.1.call-start = ((), (), s32[]{:S(2)}) async-start(), calls=%async_computation.20 | async-start | bytes 6488064 | tf_op jit(solution)/shard_map/all_gather | solution.py:124
  327.2 103.4 %all-gather.32.cloned.1.call-start = ((), (), s32[]{:S(2)}) async-start(), calls=%async_computation.21 | async-start | bytes 6488064 | tf_op jit(solution)/shard_map/all_gather | solution.py:123
  329.3 141.0 %reduce-scatter.19.cloned.1.call-start = ((), (), s32[]{:S(2)}) async-start(), calls=%async_computation.22 | async-start | bytes 589824 | tf_op jit(solution)/shard_map/reduce_scatter | solution.py:52
  489.7 87.6 %all-gather.34.cloned.1.call-start = ((), (), s32[]{:S(2)}) async-start(), calls=%async_computation.24 | async-start | bytes 6488064 | tf_op jit(solution)/shard_map/all_gather | solution.py:124
  524.4 103.4 %all-gather.36.cloned.1.call-start = ((), (), s32[]{:S(2)}) async-start(), calls=%async_computation.25 | async-start | bytes 6488064 | tf_op jit(solution)/shard_map/all_gather | solution.py:123
  526.5 138.8 %reduce-scatter.23.cloned.1.call-start = ((), (), s32[]{:S(2)}) async-start(), calls=%async_computation.26 | async-start | bytes 589824 | tf_op jit(solution)/shard_map/reduce_scatter | solution.py:52
  690.8 72.6 %all-gather.44.cloned.1.call-start = ((), (), s32[]{:S(2)}) async-start(), calls=%async_computation.38 | async-start | bytes 6488064 | tf_op jit(solution)/shard_map/all_gather | solution.py:239
  691.8 188.1 %all-gather.38.cloned.1.call-start = ((), (), s32[]{:S(2)}) async-start(), calls=%async_computation.29 | async-start | bytes 6488064 | tf_op jit(solution)/shard_map/all_gather | solution.py:240
  722.6 206.3 %reduce-scatter.29.cloned.1.call-start = ((), (), s32[]{:S(2)}) async-start(), calls=%async_computation.30 | async-start | bytes 589824 | tf_op jit(solution)/shard_map/reduce_scatter | solution.py:62
  959.5 69.2 %all-gather.46.cloned.1.call-start = ((), (), s32[]{:S(2)}) async-start(), calls=%async_computation.39 | async-start | bytes 6488064 | tf_op jit(solution)/shard_map/all_gather | solution.py:239
  960.1 177.3 %all-gather.40.cloned.1.call-start = ((), (), s32[]{:S(2)}) async-start(), calls=%async_computation.32 | async-start | bytes 6488064 | tf_op jit(solution)/shard_map/all_gather | solution.py:240
  991.0 197.2 %reduce-scatter.33.cloned.1.call-start = ((), (), s32[]{:S(2)}) async-start(), calls=%async_computation.33 | async-start | bytes 589824 | tf_op jit(solution)/shard_map/reduce_scatter | solution.py:62
  1173.0 63.7 %reduce-scatter.35.cloned.1.call-start = ((), (), s32[]{:S(2)}) async-start(), calls=%async_computation.34 | async-start | bytes 589824 | tf_op jit(solution)/shard_map/reduce_scatter | solution.py:62
  1218.8 69.3 %all-gather.48.cloned.1.call-start = ((), (), s32[]{:S(2)}) async-start(), calls=%async_computation.40 | async-start | bytes 6488064 | tf_op jit(solution)/shard_map/all_gather | solution.py:239
  1219.3 131.5 %reduce-scatter.25.cloned.1.call-start = ((), (), s32[]{:S(2)}) async-start(), calls=%async_computation.27 | async-start | bytes 589824 | tf_op jit(solution)/shard_map/reduce_scatter | solution.py:52
  1222.9 223.1 %all-gather.42.cloned.1.call-start = ((), (), s32[]{:S(2)}) async-start(), calls=%async_computation.35 | async-start | bytes 6488064 | tf_op jit(solution)/shard_map/all_gather | solution.py:240
  1251.1 237.0 %reduce-scatter.39.cloned.1.call-start = ((), (), s32[]{:S(2)}) async-start(), calls=%async_computation.37 | async-start | bytes 2433024 | tf_op jit(solution)/shard_map/reduce_scatter | solution.py:336
  1402.8 159.0 %reduce-scatter.37.cloned.1.call-start = ((), (), s32[]{:S(2)}) async-start(), calls=%async_computation.36 | async-start | bytes 589824 | tf_op jit(solution)/shard_map/reduce_scatter | solution.py:62
  1480.8 412.4 %all-reduce.7.cloned.1.call-start = ((), (), s32[]{:S(2)}) async-start(), calls=%async_computation.41 | async-start | bytes 15335424
  (187 other events, 5119.6 us)
Sparse Core Ops, SparseCore 0:
  10.4 47.2 all-gather.19
  60.0 48.6 all-gather.21
  110.9 48.1 all-gather.23
  200.2 44.2 all-gather.25
  246.8 43.5 all-gather.27
  294.1 15.9 reduce-scatter.16
  327.3 52.8 all-gather.29
  382.4 48.1 all-gather.31
  454.7 15.5 reduce-scatter.18
  489.8 17.4 reduce-scatter.20
  524.5 52.8 all-gather.33
  579.6 48.1 all-gather.35
  690.9 17.4 reduce-scatter.26
  710.5 49.1 all-gather.43
  761.8 48.5 all-gather.37
  959.7 17.7 reduce-scatter.30
  979.6 49.1 all-gather.45
  1031.0 48.1 all-gather.39
  1218.9 17.7 reduce-scatter.34
  1238.8 49.1 all-gather.47
  1308.9 49.1 all-gather.41
  1402.9 75.8 reduce-scatter.38
  1481.7 17.8 reduce-scatter.36
  1504.0 119.2 all-reduce.6
  (5 shorter events, 74.8 us)
where the time goes:
time: 1920 us; the launch traced here: 1900 us
  blocking collectives  664 us (35%)
  waiting for transfers between devices  571 us (30%)
  matrix products  316 us (16%)
  local copies, waits for them, and re-layouts  241 us (13%)
  other arithmetic  84.1 us (4%)
  between operations  19.6 us (1%)
    psum x1, blocking collectives, on_device(): sum_vector = lax.psum(grad_vector[None], ('dp', 'tensor'))  327 us
    all_gather x3, waiting for transfers between devices, on_device(): key_all = lax.all_gather(forward_key_rows, 'dp', axis=0, tiled=True)  119 us
    all_gather x3, waiting for transfers between devices, on_device(): value_all = lax.all_gather(forward_value_rows, 'dp', axis=0, tiled=True)  112 us
    gather x30, local copies, waits for them, and re-layouts, select_blocks(): whole.reshape((block_count, block_rows) + whole.shape[1:])[blocks]  99.4 us
    all_gather x3, blocking collectives, on_device(): total_all = lax.all_gather(log_total[:, :, 0].T, 'dp', axis=0, tiled=True)  79.2 us
    all_gather x3, blocking collectives, on_device(): dots_all = lax.all_gather(row_dots[:, :, 0].T, 'dp', axis=0, tiled=True)  74.2 us
    reduce_scatter x6, waiting for transfers between devices, scatter_grads(): lax.psum_scatter(values.astype(jnp.bfloat16), 'tensor', scatter_dimension...  73 us
    reduce_scatter x6, waiting for transfers between devices, scatter_rows(): lax.psum_scatter(values.astype(jnp.bfloat16), 'tensor', scatter_dimension...  68.9 us
  transfers between devices with their start and end apart: 33, of which 25 were waited for; matrix products, arithmetic and copies ran while one was open for 22% of the time, Pallas kernels for 0%

commit v1 on v0

v1 whole, which is shorter than its diff:
```python
import jax, jax.numpy as jnp
from jax import lax
from jax.experimental import pallas as pl
from jax.experimental.pallas import tpu as pltpu
from jax.sharding import Mesh, PartitionSpec as P
MESH = pl.DeviceIdType.MESH
ORDERS = ("xyz", "yzx", "zxy")


class Spot:
    def __init__(self):
        self.s, self.y, self.z, self.c, self.t = (lax.axis_index(a) for a in "syzct")
        self.x = self.t * 2 + self.s

    def at(self, axis):
        return {"x": self.x, "y": self.y, "z": self.z}[axis]

    def shifted(self, axis, by):
        return lax.rem(self.at(axis) + (by + 4), 4)

    def device(self, axis, by):
        x, y, z = self.x, self.y, self.z
        moved = self.shifted(axis, by)
        if axis == "x":
            x = moved
        elif axis == "y":
            y = moved
        else:
            z = moved
        return (lax.rem(x, 2), y, z, self.c, lax.div(x, 2))

    def sibling(self):
        return (self.s, self.y, self.z, 1 - self.c, self.t)


class Copies:
    def __init__(self, send_sems, recv_sems):
        self.send_sems, self.recv_sems, self.count = send_sems, recv_sems, 0
        self.sent = []

    def make(self, src, dst, device):
        n = self.count
        self.count += 1
        copy = pltpu.make_async_remote_copy(
            src_ref=src, dst_ref=dst, send_sem=self.send_sems.at[n], recv_sem=self.recv_sems.at[n],
            device_id=device, device_id_type=MESH)
        self.sent.append(copy)
        return copy

    def start(self, src, dst, device):
        copy = self.make(src, dst, device)
        copy.start()
        return copy

    def finish(self):
        for copy in self.sent:
            copy.wait_send()


def greet(spot, with_sibling):
    barrier = pltpu.get_barrier_semaphore()
    peers = [spot.device(axis, by) for axis in "xyz" for by in (1, -1)]
    if with_sibling:
        peers.append(spot.sibling())
    for peer in peers:
        pl.semaphore_signal(barrier, inc=1, device_id=peer, device_id_type=MESH)
    pl.semaphore_wait(barrier, len(peers))


def gather_kernel(w_ref, out_ref, send_sems, recv_sems, own_sems):
    spot = Spot()
    copies = Copies(send_sems, recv_sems)
    half = out_ref.at[spot.c]
    locals_ = []
    for k in range(3):
        local = pltpu.make_async_copy(w_ref.at[k], half.at[k, spot.x, spot.y, spot.z], own_sems.at[k])
        local.start()
        locals_.append(local)
    greet(spot, True)
    for local in locals_:
        local.wait()

    def part(k, order, phase, position, piece=None):
        axis = order[phase]
        index = {}
        for n, name in enumerate(order):
            index[name] = slice(None) if n < phase else spot.at(name)
        index[axis] = position
        rows = slice(None)
        if piece is not None:
            start, size = piece
            if phase == 0:
                rows = pl.ds(start, size)
            else:
                index[order[0]] = pl.ds(start, size)
        return half.at[k, index["x"], index["y"], index["z"], rows]

    def ring(k, order, phase, position, piece, by):
        ref = part(k, order, phase, position, piece)
        return copies.start(ref, ref, spot.device(order[phase], by))

    def push(k, order, phase, position, piece):
        ref = part(k, order, phase, position, piece)
        return copies.start(ref, ref, spot.sibling())

    pushes = []
    for phase in range(3):
        if phase == 0:
            to_right, to_left = [(0, 32), (32, 16)], [(32, 16), (0, 32)]
            pass_right, pass_left = [(0, 32)], [(32, 16)]
        elif phase == 1:
            to_right, to_left = [(0, 2), (2, 2)], [(2, 2), (0, 2)]
            pass_right, pass_left = [(0, 2)], [(2, 2)]
        else:
            to_right, to_left = [(0, 1), (1, 1), (2, 1), (3, 1)], [(2, 1), (3, 1), (0, 1), (1, 1)]
            pass_right, pass_left = [(0, 1), (1, 1)], [(2, 1), (3, 1)]
        first = {}
        for n in range(len(to_right)):
            for k, order in enumerate(ORDERS):
                me = spot.at(order[phase])
                first[k, "r", to_right[n]] = ring(k, order, phase, me, to_right[n], 1)
                first[k, "l", to_left[n]] = ring(k, order, phase, me, to_left[n], -1)
        if phase == 2:
            for k, order in enumerate(ORDERS):
                pushes.append(push(k, order, phase, spot.at(order[phase]), None))
        second = []
        for n in range(len(to_right)):
            for k, order in enumerate(ORDERS):
                axis = order[phase]
                before, after = spot.shifted(axis, -1), spot.shifted(axis, 1)
                first[k, "r", to_right[n]].wait_recv()
                if to_right[n] in pass_right:
                    second.append((k, to_right[n], ring(k, order, phase, before, to_right[n], 1)))
                first[k, "l", to_left[n]].wait_recv()
                if to_left[n] in pass_left:
                    second.append((k, to_left[n], ring(k, order, phase, after, to_left[n], -1)))
                if phase == 2:
                    pushes.append(push(k, order, phase, before, to_right[n]))
                    pushes.append(push(k, order, phase, after, to_left[n]))
        for k, piece, copy in second:
            copy.wait_recv()
            if phase == 2:
                order = ORDERS[k]
                pushes.append(push(k, order, phase, spot.shifted(order[phase], 2), piece))
    for copy in pushes:
        copy.wait_recv()
    copies.finish()


def gather_weights(w):
    return pl.pallas_call(
        gather_kernel,
        out_shape=jax.ShapeDtypeStruct((2, 3, 4, 4, 4, 48, 768), jnp.bfloat16),
        in_specs=[pl.BlockSpec(memory_space=pl.ANY)],
        out_specs=pl.BlockSpec(memory_space=pl.ANY),
        scratch_shapes=[pltpu.SemaphoreType.DMA((160,)), pltpu.SemaphoreType.DMA((160,)), pltpu.SemaphoreType.DMA((3,))],
        compiler_params=pltpu.CompilerParams(collective_id=1, has_side_effects=True),
        name="gather_weights",
    )(w)


def reduce_kernel(g_ref, out_ref, a0, b0, l0, r0, q0, a1, b1, l1, r1, q1, a2, b2, l2, r2, send_sems, recv_sems):
    spot = Spot()
    copies = Copies(send_sems, recv_sems)
    greet(spot, False)
    first_in, second_in = [(a0, b0), (a1, b1), (a2, b2)], [(l0, r0), (l1, r1), (l2, r2)]
    quarters = [q0, q1]

    def source(k, phase, order, position, piece=None):
        axis = order[phase]
        rest = order[phase + 1:]
        if phase == 0:
            index = {axis: position}
            for n, name in enumerate(rest):
                index[name] = slice(None)
            if piece is not None:
                index[max(rest)] = pl.ds(2 * piece, 2)
            return g_ref.at[k, index["x"], index["y"], index["z"]]
        held = quarters[phase - 1].at[k]
        names = [n for n in "xyz" if n in order[phase:]]
        index = []
        for name in names:
            if name == axis:
                index.append(position)
            elif piece is not None and name == rest[0]:
                index.append(pl.ds(2 * piece, 2))
            else:
                index.append(slice(None))
        rows = slice(None)
        if phase == 2 and piece is not None:
            rows = pl.ds(0, 32) if piece == 0 else pl.ds(32, 16)
        return held.at[tuple(index) + (rows,)]

    def slot(buffer, k, phase, order, piece):
        held = buffer.at[k]
        if piece is None:
            return held
        if phase == 2:
            return held.at[pl.ds(0, 32) if piece == 0 else pl.ds(32, 16)]
        rest = order[phase + 1:]
        names = [n for n in "xyz" if n in rest]
        return held.at[tuple(pl.ds(2 * piece, 2) if n == max(rest) else slice(None) for n in names)]

    def each(shape, body):
        lead = shape[:-2]
        if not lead:
            body(())
        elif len(lead) == 1:
            @pl.loop(0, lead[0])
            def _(i):
                body((i,))
        else:
            @pl.loop(0, lead[0])
            def _(i):
                @pl.loop(0, lead[1])
                def _(j):
                    body((i, j))

    for phase in range(3):
        started = []
        for k, gathered in enumerate(ORDERS):
            order = gathered[::-1]
            axis = order[phase]
            right, left = spot.device(axis, 1), spot.device(axis, -1)
            a, b = first_in[phase]
            l, r = second_in[phase]
            far = spot.shifted(axis, 2)
            ca = copies.start(source(k, phase, order, far, 0), a.at[k], right)
            cb = copies.start(source(k, phase, order, far, 1), b.at[k], left)
            started.append([ca, cb])
        for k, gathered in enumerate(ORDERS):
            order = gathered[::-1]
            axis = order[phase]
            right, left = spot.device(axis, 1), spot.device(axis, -1)
            l, r = second_in[phase]
            after, before = spot.shifted(axis, 1), spot.shifted(axis, -1)
            started[k].append(copies.start(source(k, phase, order, after, 1), slot(l, k, phase, order, 1), right))
            started[k].append(copies.start(source(k, phase, order, before, 0), slot(r, k, phase, order, 0), left))
        for k, gathered in enumerate(ORDERS):
            order = gathered[::-1]
            axis = order[phase]
            right, left = spot.device(axis, 1), spot.device(axis, -1)
            a, b = first_in[phase]
            l, r = second_in[phase]
            after, before = spot.shifted(axis, 1), spot.shifted(axis, -1)

            def join(buffer, own):
                def body(i):
                    buffer[i] = (buffer[i].astype(jnp.float32) + own[i].astype(jnp.float32)).astype(jnp.bfloat16)
                each(buffer.shape, body)

            started[k][0].wait_recv()
            join(a.at[k], source(k, phase, order, after, 0))
            started[k].append(copies.start(a.at[k], slot(l, k, phase, order, 0), right))
            started[k][1].wait_recv()
            join(b.at[k], source(k, phase, order, before, 1))
            started[k].append(copies.start(b.at[k], slot(r, k, phase, order, 1), left))
        for k, gathered in enumerate(ORDERS):
            order = gathered[::-1]
            axis = order[phase]
            l, r = second_in[phase]
            for copy in started[k][2:]:
                copy.wait_recv()
            own = source(k, phase, order, spot.at(axis))
            left_in, right_in = l.at[k], r.at[k]
            target = out_ref.at[k] if phase == 2 else quarters[phase].at[k]

            def body(i):
                target[i] = (own[i].astype(jnp.float32) + left_in[i].astype(jnp.float32)
                             + right_in[i].astype(jnp.float32)).astype(target.dtype)
            each(target.shape, body)
    copies.finish()


def reduce_grads(g):
    low = lambda *s: pltpu.VMEM(s, jnp.bfloat16)
    return pl.pallas_call(
        reduce_kernel,
        out_shape=jax.ShapeDtypeStruct((3, 48, 768), jnp.float32),
        in_specs=[pl.BlockSpec(memory_space=pltpu.VMEM)],
        out_specs=pl.BlockSpec(memory_space=pltpu.VMEM),
        scratch_shapes=[
            low(3, 4, 2, 48, 768), low(3, 4, 2, 48, 768), low(3, 4, 4, 48, 768), low(3, 4, 4, 48, 768), low(3, 4, 4, 48, 768),
            low(3, 2, 48, 768), low(3, 2, 48, 768), low(3, 4, 48, 768), low(3, 4, 48, 768), low(3, 4, 48, 768),
            low(3, 32, 768), low(3, 16, 768), low(3, 48, 768), low(3, 48, 768),
            pltpu.SemaphoreType.DMA((60,)), pltpu.SemaphoreType.DMA((60,)),
        ],
        compiler_params=pltpu.CompilerParams(collective_id=2, has_side_effects=True, vmem_limit_bytes=56 * 2**20),
        name="reduce_grads",
    )(g)


def lanes_swapped(tile):
    return pltpu.roll(tile, 64, 1)


def split_pair(ref, column):
    top = ref[0:64, column:column + 128].astype(jnp.float32)
    low = ref[64:128, column:column + 128].astype(jnp.float32)
    left = lax.broadcasted_iota(jnp.int32, (64, 128), 1) < 64
    first = jnp.where(left, top, lanes_swapped(low))
    second = jnp.where(left, lanes_swapped(top), low)
    return first.astype(jnp.bfloat16), second.astype(jnp.bfloat16)


def join_pair(first, second):
    first, second = first.astype(jnp.float32), second.astype(jnp.float32)
    left = lax.broadcasted_iota(jnp.int32, (64, 128), 1) < 64
    top = jnp.where(left, first, lanes_swapped(second))
    low = jnp.where(left, lanes_swapped(first), second)
    return top.astype(jnp.bfloat16), low.astype(jnp.bfloat16)


def pack_rows(block):
    return jnp.concatenate([block[0:64], block[64:128]], axis=1)


class Group:
    def __init__(self):
        self.s, self.y, self.z, self.c, self.t = (lax.axis_index(a) for a in "syzct")
        self.me = self.z * 4 + self.c * 2 + self.t
        self.active = jnp.logical_or(self.c == 0, lax.rem(self.z + self.t, 2) == 0)
        self.head = jnp.where(self.c == 0, self.z * 2 + self.t, 8 + self.z)

    def member(self, index):
        return (self.s, self.y, lax.div(index, 4), lax.rem(lax.div(index, 2), 2), lax.rem(index, 2))

    def holder(self, head):
        late = head - 8
        return jnp.where(head < 8, lax.div(head, 2) * 4 + lax.rem(head, 2), late * 4 + 2 + lax.rem(late, 2))

    def greet(self):
        barrier = pltpu.get_barrier_semaphore()

        @pl.loop(1, 16)
        def _(n):
            pl.semaphore_signal(barrier, inc=1, device_id=self.member(lax.rem(self.me + n, 16)), device_id_type=MESH)
        pl.semaphore_wait(barrier, 15)


def out_to_heads(group, packed, landed, send_sems, recv_sems):
    @pl.loop(0, 12)
    def _(n):
        head = lax.rem(group.me + n, 12)
        target = group.holder(head)

        @pl.when(target != group.me)
        def _():
            pltpu.make_async_remote_copy(
                src_ref=packed.at[head], dst_ref=landed.at[group.me], send_sem=send_sems.at[head],
                recv_sem=recv_sems.at[group.me], device_id=group.member(target), device_id_type=MESH).start()

    @pl.when(group.active)
    def _():
        landed[group.me] = packed[group.head]


def await_member(group, packed, landed, send_sems, recv_sems, index):
    @pl.when(group.me != index)
    def _():
        pltpu.make_async_remote_copy(
            src_ref=packed.at[0], dst_ref=landed.at[index], send_sem=send_sems.at[0],
            recv_sem=recv_sems.at[index], device_id=group.member(index), device_id_type=MESH).wait_recv()


def sent_to_heads(group, packed, landed, send_sems, recv_sems):
    @pl.loop(0, 12)
    def _(head):
        @pl.when(group.holder(head) != group.me)
        def _():
            pltpu.make_async_remote_copy(
                src_ref=packed.at[head], dst_ref=landed.at[group.me], send_sem=send_sems.at[head],
                recv_sem=recv_sems.at[group.me], device_id=group.member(group.holder(head)),
                device_id_type=MESH).wait_send()


def back_to_member(group, packed, landed, send_sems, recv_sems, index):
    @pl.when(group.me != index)
    def _():
        pltpu.make_async_remote_copy(
            src_ref=packed.at[index], dst_ref=landed.at[group.head], send_sem=send_sems.at[index],
            recv_sem=recv_sems.at[group.head], device_id=group.member(index), device_id_type=MESH).start()

    @pl.when(group.me == index)
    def _():
        landed[group.head] = packed[index]


def finish_back(group, packed, landed, send_sems, recv_sems):
    @pl.when(group.active)
    def _():
        @pl.loop(0, 16)
        def _(index):
            @pl.when(group.me != index)
            def _():
                pltpu.make_async_remote_copy(
                    src_ref=packed.at[index], dst_ref=landed.at[group.head], send_sem=send_sems.at[index],
                    recv_sem=recv_sems.at[group.head], device_id=group.member(index),
                    device_id_type=MESH).wait_send()

    @pl.loop(0, 12)
    def _(head):
        holder = group.holder(head)

        @pl.when(holder != group.me)
        def _():
            pltpu.make_async_remote_copy(
                src_ref=packed.at[0], dst_ref=landed.at[head], send_sem=send_sems.at[0],
                recv_sem=recv_sems.at[head], device_id=group.member(holder), device_id_type=MESH).wait_recv()


def dot_right(left, right):
    return lax.dot_general(left, right, (((1,), (1,)), ((), ())), preferred_element_type=jnp.float32)


def dot(left, right):
    return jnp.dot(left, right, preferred_element_type=jnp.float32)


def masked_scores(scores, block):
    key = lax.broadcasted_iota(jnp.int32, scores.shape, 0)
    query = lax.broadcasted_iota(jnp.int32, scores.shape, 1) + block * 256
    return jnp.where(key <= query, scores, -1e30)


def attend_kernel(q_ref, k_ref, v_ref, mixed_ref, heads_ref, total_ref,
                  packed, landed, back, home, value_turned, send_a, recv_a, send_b, recv_b):
    group = Group()
    for n, ref in enumerate((q_ref, k_ref, v_ref)):
        for pair in range(6):
            first, second = split_pair(ref, pair * 128)
            packed[2 * pair, n * 64:n * 64 + 64] = first
            packed[2 * pair + 1, n * 64:n * 64 + 64] = second
    group.greet()
    out_to_heads(group, packed, landed, send_a, recv_a)

    @pl.when(group.active)
    def _():
        for block in range(8):
            for index in (2 * block, 2 * block + 1):
                await_member(group, packed, landed, send_a, recv_a, index)
                for n in range(3):
                    tile = landed[index, n * 64:n * 64 + 64]
                    heads_ref[n, index * 128:index * 128 + 64] = tile[:, 0:64]
                    heads_ref[n, index * 128 + 64:index * 128 + 128] = tile[:, 64:128]
            rows = slice(block * 256, block * 256 + 256)
            value_turned[:, rows] = heads_ref[2, rows].T
            count = block * 256 + 256
            scores = masked_scores(dot_right(heads_ref[1, 0:count], heads_ref[0, rows]), block)
            largest = jnp.max(scores, axis=0, keepdims=True)
            weights = jnp.exp(scores - largest)
            total = jnp.sum(weights, axis=0, keepdims=True)
            total_ref[block:block + 1, :] = largest + jnp.log(total)
            mixed = dot(value_turned[:, 0:count], weights.astype(jnp.bfloat16)) / total
            mixed = mixed.T
            for n, index in enumerate((2 * block, 2 * block + 1)):
                back[index] = pack_rows(mixed[n * 128:n * 128 + 128]).astype(jnp.bfloat16)
                back_to_member(group, back, home, send_b, recv_b, index)

    sent_to_heads(group, packed, landed, send_a, recv_a)
    finish_back(group, back, home, send_b, recv_b)
    for pair in range(6):
        top, low = join_pair(home[2 * pair], home[2 * pair + 1])
        mixed_ref[0:64, pair * 128:pair * 128 + 128] = top
        mixed_ref[64:128, pair * 128:pair * 128 + 128] = low


def attend(q, k, v, which):
    low = lambda *s: pltpu.VMEM(s, jnp.bfloat16)
    vmem = pl.BlockSpec(memory_space=pltpu.VMEM)
    return pl.pallas_call(
        attend_kernel,
        out_shape=(jax.ShapeDtypeStruct((128, 768), jnp.bfloat16), jax.ShapeDtypeStruct((3, 2048, 64), jnp.bfloat16),
                   jax.ShapeDtypeStruct((8, 256), jnp.float32)),
        in_specs=[vmem] * 3,
        out_specs=(vmem, vmem, vmem),
        scratch_shapes=[
            low(12, 192, 128), low(16, 192, 128), low(16, 64, 128), low(12, 64, 128), low(64, 2048),
            pltpu.SemaphoreType.DMA((12,)), pltpu.SemaphoreType.DMA((16,)),
            pltpu.SemaphoreType.DMA((16,)), pltpu.SemaphoreType.DMA((12,)),
        ],
        compiler_params=pltpu.CompilerParams(collective_id=3 + which, has_side_effects=True, vmem_limit_bytes=48 * 2**20),
        name="attend",
    )(q, k, v)


def attend_back_kernel(grad_ref, heads_ref, total_ref, dq_ref, dk_ref, dv_ref,
                       packed, landed, back, home, grad_heads, key_turned, key_sum, value_sum,
                       send_a, recv_a, send_b, recv_b):
    group = Group()
    for pair in range(6):
        first, second = split_pair(grad_ref, pair * 128)
        packed[2 * pair] = first
        packed[2 * pair + 1] = second
    group.greet()
    out_to_heads(group, packed, landed, send_a, recv_a)

    @pl.when(group.active)
    def _():
        key_turned[...] = heads_ref[1].T
        for block in reversed(range(8)):
            for index in (2 * block, 2 * block + 1):
                await_member(group, packed, landed, send_a, recv_a, index)
                tile = landed[index]
                grad_heads[index * 128:index * 128 + 64] = tile[:, 0:64]
                grad_heads[index * 128 + 64:index * 128 + 128] = tile[:, 64:128]
            rows = slice(block * 256, block * 256 + 256)
            count = block * 256 + 256
            query, grad = heads_ref[0, rows], grad_heads[rows]
            scores = masked_scores(dot_right(heads_ref[1, 0:count], query), block)
            weights = jnp.exp(scores - total_ref[block:block + 1, :])
            soft = dot_right(heads_ref[2, 0:count], grad)
            dots = jnp.sum(weights * soft, axis=0, keepdims=True)
            moved = (weights * (soft - dots)).astype(jnp.bfloat16)
            for_key, for_value = dot(moved, query), dot(weights.astype(jnp.bfloat16), grad)
            if block == 7:
                key_sum[...] = for_key
                value_sum[...] = for_value
            else:
                key_sum[0:count] = key_sum[0:count] + for_key
                value_sum[0:count] = value_sum[0:count] + for_value
            for_query = dot(key_turned[:, 0:count], moved).T.astype(jnp.bfloat16).astype(jnp.float32) * 0.125
            for n, index in enumerate((2 * block, 2 * block + 1)):
                part = slice(index * 128, index * 128 + 128)
                back[index, 0:64] = pack_rows(for_query[n * 128:n * 128 + 128]).astype(jnp.bfloat16)
                back[index, 64:128] = pack_rows(key_sum[part]).astype(jnp.bfloat16)
                back[index, 128:192] = pack_rows(value_sum[part]).astype(jnp.bfloat16)
                back_to_member(group, back, home, send_b, recv_b, index)

    sent_to_heads(group, packed, landed, send_a, recv_a)
    finish_back(group, back, home, send_b, recv_b)
    for n, ref in enumerate((dq_ref, dk_ref, dv_ref)):
        for pair in range(6):
            top, low = join_pair(home[2 * pair, n * 64:n * 64 + 64], home[2 * pair + 1, n * 64:n * 64 + 64])
            ref[0:64, pair * 128:pair * 128 + 128] = top
            ref[64:128, pair * 128:pair * 128 + 128] = low


def attend_back(grad, heads, total, which):
    low = lambda *s: pltpu.VMEM(s, jnp.bfloat16)
    vmem = pl.BlockSpec(memory_space=pltpu.VMEM)
    return pl.pallas_call(
        attend_back_kernel,
        out_shape=(jax.ShapeDtypeStruct((128, 768), jnp.bfloat16),) * 3,
        in_specs=[vmem] * 3,
        out_specs=(vmem,) * 3,
        scratch_shapes=[
            low(12, 64, 128), low(16, 64, 128), low(16, 192, 128), low(12, 192, 128), low(2048, 64), low(64, 2048),
            pltpu.VMEM((2048, 64), jnp.float32), pltpu.VMEM((2048, 64), jnp.float32),
            pltpu.SemaphoreType.DMA((12,)), pltpu.SemaphoreType.DMA((16,)),
            pltpu.SemaphoreType.DMA((16,)), pltpu.SemaphoreType.DMA((12,)),
        ],
        compiler_params=pltpu.CompilerParams(collective_id=5 + which, has_side_effects=True, vmem_limit_bytes=48 * 2**20),
        name="attend_back",
    )(grad, heads, total)


def move_kernel(order_ref, x_ref, out_ref, middle, turned, send_a, recv_a, send_b, recv_b):
    s, y, z, c, t = (lax.axis_index(a) for a in "syzct")
    me = y * 8 + z * 2 + c

    def member(index):
        return (s, lax.div(index, 8), lax.rem(lax.div(index, 2), 4), lax.rem(index, 2), t)

    barrier = pltpu.get_barrier_semaphore()

    @pl.loop(1, 32)
    def _(n):
        pl.semaphore_signal(barrier, inc=1, device_id=member(lax.rem(me + n, 32)), device_id_type=MESH)
    pl.semaphore_wait(barrier, 31)

    def exchange(source, target, send_sems, recv_sems):
        def copy(n):
            to = lax.rem(me + n, 32)
            return pltpu.make_async_remote_copy(
                src_ref=source.at[to], dst_ref=target.at[me], send_sem=send_sems.at[n], recv_sem=recv_sems.at[n],
                device_id=member(to), device_id_type=MESH)

        @pl.loop(1, 32)
        def _(n):
            copy(n).start()
        target[me] = source[me]

        @pl.loop(1, 32)
        def _(n):
            came = lax.rem(me + 32 - n, 32)
            pltpu.make_async_remote_copy(
                src_ref=source.at[came], dst_ref=target.at[came], send_sem=send_sems.at[n], recv_sem=recv_sems.at[n],
                device_id=member(came), device_id_type=MESH).wait_recv()
        return copy

    first = exchange(x_ref, middle, send_a, recv_a)

    @pl.loop(0, 32)
    def _(n):
        turned[n] = middle[order_ref[n]]
    second = exchange(turned, out_ref, send_b, recv_b)

    @pl.loop(1, 32)
    def _(n):
        first(n).wait_send()
        second(n).wait_send()


def move_blocks(order, x, which):
    vmem = pl.BlockSpec(memory_space=pltpu.VMEM)
    sems = [pltpu.SemaphoreType.DMA((32,))] * 4
    return pl.pallas_call(
        move_kernel,
        out_shape=jax.ShapeDtypeStruct(x.shape, x.dtype),
        in_specs=[pl.BlockSpec(memory_space=pltpu.SMEM), vmem],
        out_specs=vmem,
        scratch_shapes=[pltpu.VMEM(x.shape, x.dtype), pltpu.VMEM(x.shape, x.dtype)] + sems,
        compiler_params=pltpu.CompilerParams(collective_id=which, has_side_effects=True),
        name="move_blocks",
    )(order, x)


def deltas_kernel(left_a, left_b, right_ref, out_ref):
    def product(left):
        return lax.dot_general(left, right_ref[0, 0, 0], (((0,), (0,)), ((), ())), preferred_element_type=jnp.float32)
    which = pl.program_id(1)
    first = product(left_a[0, 0])
    out_ref[0, 0] = first.astype(jnp.bfloat16)

    @pl.when(which == 1)
    def _():
        out_ref[0, 0, :, 384:768] = product(left_b[0, 0])[:, 384:768].astype(jnp.bfloat16)


def weight_deltas(left, right):
    def left_a(layer, part, half):
        return (layer, jnp.where(part == 2, 3, part), 0, 0)

    def left_b(layer, part, half):
        return (layer, jnp.where(part == 2, 3, part * 2), 0, 0)
    return pl.pallas_call(
        deltas_kernel,
        grid=(2, 3, 2),
        out_shape=jax.ShapeDtypeStruct((3, 4, 768, 768), jnp.bfloat16),
        in_specs=[
            pl.BlockSpec((1, 1, 256, 768), left_a), pl.BlockSpec((1, 1, 256, 768), left_b),
            pl.BlockSpec((1, 1, 1, 256, 768), lambda layer, part, half: (layer, part, half, 0, 0)),
        ],
        out_specs=pl.BlockSpec((1, 1, 768, 768), lambda layer, part, half: (part, half * 2 + layer, 0, 0)),
        compiler_params=pltpu.CompilerParams(vmem_limit_bytes=32 * 2**20),
        name="weight_deltas",
    )(left, left, right)


epsilon = 1e-05


def normalize(residual, gain_row, shift_row):
    average = jnp.mean(residual, axis=-1, keepdims=True)
    centred = residual - average
    spread = jnp.mean(centred * centred, axis=-1, keepdims=True)
    return centred * lax.rsqrt(spread + epsilon) * gain_row + shift_row


def smooth_gate(values):
    return jax.nn.gelu(values, approximate=False)


def swap(value, axis):
    return lax.ppermute(value, axis, [(0, 1), (1, 0)])


def low(value):
    return value.astype(jnp.bfloat16)


def layer_forward(entering, weights, bias_qv, bias_up, rows, layer):
    pair_qk, pair_vo, up_a, up_b, down_a, down_b = weights
    normed = low(normalize(entering, rows[0], rows[1]))
    qk = [dot(normed, pair_qk[t]) for t in range(2)]
    query = jnp.concatenate([qk[t][:, :384] for t in range(2)], axis=1)
    key = low(jnp.concatenate([qk[t][:, 384:] for t in range(2)], axis=1))
    value = jnp.concatenate([dot(normed, pair_vo[t][:, :384]) for t in range(2)], axis=1)
    query = low((query + bias_qv[0]) * 0.125)
    value = low(value + bias_qv[1])
    mixed, heads, total = attend(query, key, value, layer)
    hidden = entering + rows[2] + sum(
        dot_right(mixed[:, t * 384:t * 384 + 384], pair_vo[t][:, 384:]) for t in range(2))
    normed_two = low(normalize(hidden, rows[3], rows[4]))
    pre = [[dot(normed_two, up[t]) + bias_up[t, n * 768:n * 768 + 768] for n, up in enumerate((up_a, up_b))] for t in range(2)]
    active = [[low(smooth_gate(p)) for p in two] for two in pre]
    leaving = hidden + rows[5] + sum(
        dot_right(active[t][n], down[t]) for t in range(2) for n, down in enumerate((down_a, down_b)))
    return leaving, (entering, normed, mixed, heads, total, hidden, normed_two, pre, active)


def layer_backward(arriving, kept, weights, rows, layer):
    pair_qk, pair_vo, up_a, up_b, down_a, down_b = weights
    entering, normed, mixed, heads, total, hidden, normed_two, pre, active = kept
    carried = arriving.astype(jnp.float32)
    grad_pre = [[None, None], [None, None]]
    for t in range(2):
        for n, down in enumerate((down_a, down_b)):
            grad_active = dot(arriving, down[t])
            grad_pre[t][n] = low(jax.vjp(smooth_gate, pre[t][n])[1](grad_active)[0])
    grad_normed_two = sum(
        dot_right(grad_pre[t][n], up[t]) for t in range(2) for n, up in enumerate((up_a, up_b)))
    through_two, gain_two, shift_two = jax.vjp(normalize, hidden, rows[3], rows[4])[1](grad_normed_two)
    grad_hidden = carried + through_two
    hidden_low = low(grad_hidden)
    grad_mixed = low(jnp.concatenate([dot(hidden_low, pair_vo[t][:, 384:]) for t in range(2)], axis=1))
    grad_q, grad_k, grad_v = attend_back(grad_mixed, heads, total, layer)
    grad_normed = 0.0
    for t in range(2):
        cut = slice(t * 384, t * 384 + 384)
        grad_normed += dot_right(jnp.concatenate([grad_q[:, cut], grad_k[:, cut]], axis=1), pair_qk[t])
        grad_normed += dot_right(grad_v[:, cut], pair_vo[t][:, :384])
    through_one, gain_one, shift_one = jax.vjp(normalize, entering, rows[0], rows[1])[1](grad_normed)
    grad_input = grad_hidden + through_one

    def column_sum(value):
        return jnp.sum(value.astype(jnp.float32), axis=0)
    vectors = jnp.concatenate([
        gain_one, shift_one, column_sum(hidden_low), gain_two, shift_two, column_sum(carried),
        column_sum(grad_q), column_sum(grad_v),
    ] + [column_sum(grad_pre[t][n]) for t in range(2) for n in range(2)])
    return grad_input, vectors, (normed, hidden_low, normed_two, arriving, grad_q, grad_k, grad_v, mixed, grad_pre, active)


def delta_operands(parts, core):
    normed, hidden_low, normed_two, arriving, grad_q, grad_k, grad_v, mixed, grad_pre, active = parts

    def operands(core):
        pick = lambda a, b: jnp.where(core == 0, a, b)
        left = jnp.stack([pick(normed, normed_two), pick(normed, arriving), pick(hidden_low, arriving), pick(normed_two, arriving)])
        right = []
        cuts = [slice(t * 384, t * 384 + 384) for t in range(2)]
        right.append(jnp.stack([pick(jnp.concatenate([grad_q[:, cuts[t]], grad_k[:, cuts[t]]], axis=1), grad_pre[t][1]) for t in range(2)]))
        right.append(jnp.stack([pick(jnp.concatenate([grad_v[:, cuts[t]], mixed[:, cuts[t]]], axis=1), active[t][0]) for t in range(2)]))
        right.append(jnp.stack([pick(grad_pre[t][0], active[t][1]) for t in range(2)]))
        return left, jnp.stack(right)
    own = operands(core)
    other = swap(operands(1 - core), "c")
    return tuple(jnp.concatenate([a, b], axis=-2) for a, b in zip(own, other))


def on_device(tokens_in, cotangent, place, w_qkv, w_out, w_up, w_down, qv_bias, up_bias, vectors):
    section = lax.axis_index("s")
    core = lax.axis_index("c")
    half = lax.axis_index("t")
    inverse = jnp.sum(
        jnp.where(place[None, :] == jnp.arange(32, dtype=jnp.int32)[:, None], jnp.arange(32, dtype=jnp.int32)[None, :], 0),
        axis=1)

    shard = jnp.stack([
        jnp.concatenate([w_qkv[0, 0], w_qkv[0, 1]], axis=1), jnp.concatenate([w_qkv[0, 2], w_out[0].T], axis=1),
        w_up[0, :, :768], w_up[0, :, 768:], w_down[0, :768].T, w_down[0, 768:].T])
    own = jnp.where(core == 0, shard[:3], shard[3:])
    got = swap(jnp.where(core == 0, shard[3:], shard[:3]), "c")
    both = jnp.where(core == 0, jnp.concatenate([own, got], axis=1), jnp.concatenate([got, own], axis=1))
    gathered = gather_weights(both).reshape(6, 4, 768, 768)
    weights = [[[gathered[part, t * 2 + layer] for t in range(2)] for part in range(6)] for layer in range(2)]

    small = jnp.concatenate([
        vectors[0].astype(jnp.float32).reshape(-1),
        jnp.zeros((2, 2, 384), jnp.float32).at[:, half].set(qv_bias[0].reshape(2, 384).astype(jnp.float32)).reshape(-1) * 1.0,
        jnp.zeros((2, 1536), jnp.float32).at[half].set(up_bias[0].astype(jnp.float32)).reshape(-1),
    ])
    split = jnp.arange(4608 + 1536 + 3072) >= 4608
    partner = swap(small, "t")
    small = jnp.where(split, small + partner, small)
    beside = swap(small, "s")
    small = jnp.where(section == 0, jnp.stack([small, beside]), jnp.stack([beside, small]))
    rows = small[:, :4608].reshape(2, 6, 768)
    bias_qv = small[:, 4608:6144].reshape(2, 2, 768)
    bias_up = small[:, 6144:].reshape(2, 2, 1536)

    mine = jnp.stack([jnp.where(section == 0, a[0], a[1]) for a in (tokens_in, cotangent)])
    mine = mine.reshape(2, 32, 4, 768).transpose(1, 0, 2, 3).reshape(32, 48, 128)
    mine = move_blocks(inverse, mine, 7)
    mine = mine.reshape(32, 2, 4, 768).transpose(1, 0, 2, 3).reshape(2, 128, 768)

    acts, kept = [], []
    entering = mine[0]
    for layer in range(2):
        leaving, state = layer_forward(entering.astype(jnp.float32), weights[layer], bias_qv[layer], bias_up[layer], rows[layer], layer)
        entering = low(leaving)
        acts.append(entering)
        kept.append(state)
    arriving = mine[1]
    input_grads, sums, operands = [None] * 2, [None] * 2, [None] * 2
    for layer in (1, 0):
        grad_input, sums[layer], parts = layer_backward(arriving, kept[layer], weights[layer], rows[layer], layer)
        operands[layer] = delta_operands(parts, core)
        arriving = low(grad_input)
        input_grads[layer] = arriving
    left, right = (jnp.stack(both) for both in zip(*operands))
    deltas = weight_deltas(left, right).reshape(3, 4, 4, 4, 48, 768)
    summed = reduce_grads(deltas)
    own_rows = lax.dynamic_slice_in_dim(summed, core * 24, 24, 1)
    got = swap(lax.dynamic_slice_in_dim(summed, (1 - core) * 24, 24, 1), "c")
    full = jnp.where(core == 0, jnp.concatenate([own_rows, got]), jnp.concatenate([got, own_rows]))
    grad_qkv = jnp.stack([full[0, :, :384], full[0, :, 384:], full[1, :, :384]])[None]
    grad_out = full[1, :, 384:].T[None]
    grad_up = jnp.concatenate([full[2], full[3]], axis=1)[None]
    grad_down = jnp.concatenate([full[4].T, full[5].T], axis=0)[None]

    total = lax.psum(jnp.stack(sums), ("s", "y", "z", "c", "t"))
    total = jnp.where(section == 0, total[0], total[1])
    grad_vectors = total[:4608].reshape(1, 6, 768)
    grad_qv = lax.dynamic_slice_in_dim(total[4608:6144].reshape(2, 768), half * 384, 384, 1)[None]
    grad_up_bias = lax.dynamic_slice_in_dim(total[6144:], half * 1536, 1536)[None]

    held = jnp.stack([jnp.stack([acts[layer], input_grads[layer]]) for layer in range(2)])
    stays = jnp.where(section == 0, held[0], held[1])
    came = swap(jnp.where(section == 0, held[1], held[0]), "s")
    rows_out = jnp.where(section == 0, jnp.stack([stays, came]), jnp.stack([came, stays]))
    rows_out = rows_out.reshape(4, 32, 4, 768).transpose(1, 0, 2, 3).reshape(32, 96, 128)
    rows_out = move_blocks(place, rows_out, 8)
    rows_out = rows_out.reshape(32, 4, 4, 768).transpose(1, 0, 2, 3).reshape(2, 2, 128, 768)
    acts_out = rows_out[:, 0][None]
    grads_out = rows_out[:, 1].astype(jnp.float32)[None]
    return acts_out, grads_out, grad_qkv, grad_out, grad_up, grad_down, grad_qv, grad_up_bias, grad_vectors


def solution(mesh):
    fine = Mesh(mesh.devices.reshape(2, 4, 4, 2, 2), ("s", "y", "z", "c", "t"))
    dp = ("y", "z", "c")
    blocks = P(None, dp + ("t",), None)
    weights = (P("s", None, dp, "t"), P("s", "t", dp), P("s", dp, "t"), P("s", "t", dp))
    small = (P("s", None, "t"), P("s", "t"), P("s", None, None))
    rows = P("s", None, dp + ("t",), None)
    return jax.shard_map(
        on_device, mesh=fine,
        in_specs=(blocks, blocks, P()) + weights + small,
        out_specs=(rows, rows) + weights + small,
        check_vma=False)
```

time: 1920 us -> 641 us (0.33)
  blocking collectives: 664 us -> 0 us
  waiting for transfers between devices: 571 us -> 135 us
  Pallas kernels: 0 us -> 313 us
  matrix products: 316 us -> 84.7 us
  local copies, waits for them, and re-layouts: 241 us -> 24.2 us
  other arithmetic: 84.1 us -> 43.1 us
    all_gather x15 -> x0, waiting for transfers between devices: 406 us -> none  [the longest x3 119 us: on_device(): key_all = lax.all_gather(forward_key_rows, 'dp', axis=0, tiled=True)]
    psum x2 -> x0, blocking collectives: 392 us -> none  [the longest x1 327 us: on_device(): sum_vector = lax.psum(grad_vector[None], ('dp', 'tensor'))]
    pallas_call x0 -> x9, Pallas kernels: none -> 313 us  [the longest x1 73.1 us: gather_weights(): pl.pallas_call(gather_kernel, out_shape=jax.ShapeDtypeStruct((2, 3, 4, 4,...]
    all_gather x19 -> x0, blocking collectives: 272 us -> none  [the longest x3 79.2 us: on_device(): total_all = lax.all_gather(log_total[:, :, 0].T, 'dp', axis=0, tiled=True)]
    dot_general x78 -> x56, matrix products: 316 us -> 84.7 us  [the longest x28 45.1 us: dot(): return jnp.dot(left, right, preferred_element_type=jnp.float32)]
    reduce_scatter x13 -> x0, waiting for transfers between devices: 142 us -> none  [the longest x6 73 us: scatter_grads(): lax.psum_scatter(values.astype(jnp.bfloat16), 'tensor', scatter_dimension...]
    psum x0 -> x1, waiting for transfers between devices: none -> 133 us  [on_device(): total = lax.psum(jnp.stack(sums), ('s', 'y', 'z', 'c', 't'))]
    gather x30 -> x0, local copies, waits for them, and re-layouts: 99.4 us -> none  [select_blocks(): whole.reshape((block_count, block_rows) + whole.shape[1:])[blocks]]
  transfers between devices with their start and end apart: 33 -> 10, of which waited for: 25 -> 2; matrix products, arithmetic and copies ran while one was open for 22% -> 5% of each run, Pallas kernels for 0% -> 9%
where the time goes in v1:
time: 641 us; the launch traced here: 629 us
  Pallas kernels  313 us (49%)
  waiting for transfers between devices  135 us (21%)
  matrix products  84.7 us (13%)
  other arithmetic  43.1 us (7%)
  local copies, waits for them, and re-layouts  24.2 us (4%)
  between operations  15.9 us (2%)
  starting transfers between devices  13 us (2%)
    psum x1, waiting for transfers between devices, on_device(): total = lax.psum(jnp.stack(sums), ('s', 'y', 'z', 'c', 't'))  133 us
    pallas_call x1, Pallas kernels, gather_weights(): pl.pallas_call(gather_kernel, out_shape=jax.ShapeDtypeStruct((2, 3, 4, 4,...  73.1 us
    pallas_call x1, Pallas kernels, reduce_grads(): pl.pallas_call(reduce_kernel, out_shape=jax.ShapeDtypeStruct((3, 48, 768)...  68.6 us
    pallas_call x2, Pallas kernels, attend_back(): pl.pallas_call(attend_back_kernel, out_shape=(jax.ShapeDtypeStruct((128,...  58.6 us
    pallas_call x2, Pallas kernels, move_blocks(): pl.pallas_call(move_kernel, out_shape=jax.ShapeDtypeStruct(x.shape, x.dty...  56.7 us
    pallas_call x2, Pallas kernels, attend(): pl.pallas_call(attend_kernel, out_shape=(jax.ShapeDtypeStruct((128, 768),...  48.5 us
    dot_general x28, matrix products, dot(): return jnp.dot(left, right, preferred_element_type=jnp.float32)  45.1 us
    dot_general x28, matrix products, dot_right(): lax.dot_general(left, right, (((1,), (1,)), ((), ())), preferred_element_...  39.6 us
  transfers between devices with their start and end apart: 10, of which 2 were waited for; matrix products, arithmetic and copies ran while one was open for 5% of the time, Pallas kernels for 9%

profile of v1, /device:TPU:1, one launch (start us, length us, event | category | flops | bytes accessed | tf_op | source)
XLA Modules:
  0.0 629.1 jit_solution(11361870699182136982)
XLA Ops:
  13.6 3.7 collective-permute-start
  25.2 25.1 %move_blocks.2 = bf16[32,48,128]{2,1,0:T(8,128)(2,1)} custom-call(s32[32]{0:T(128)} %select_reduce_fusion.order_ref, bf16[32,48,128]{2,1,0:T(8,128)(2,1)} %reshape.450.x_ref), custom_call_target="tpu_custom_call" | custom-call | tf_op jit(solution)/shard_map/move_blocks/pallas_call | solution.py:608
  56.6 73.1 %gather_weights.1 = bf16[2,3,4,4,4,48,768]{6,5,4,3,2,1,0:T(8,128)(2,1)} custom-call(bf16[3,48,768]{2,1,0:T(8,128)(2,1)} %maximum_select_fusion.4.w_ref), custom_call_target="tpu_custom_call" | custom-call | tf_op jit(solution)/shard_map/gather_weights/pallas_call | solution.py:151
  129.7 2.6 slice_bitcast_fusion.9
  137.2 22.2 %attend.2 = (bf16[128,768]{1,0:T(8,128)(2,1)S(1)}, bf16[3,2048,64]{2,1,0:T(8,128)(2,1)S(1)}, f32[8,256]{1,0:T(8,128)S(1)}) custom-call(bf16[128,768]{1,0:T(8,128)(2,1)S(1)} %fusion.71.q_ref, bf16[128,768]{1,0:T(8,128)(2,1)S(1)} %pad_maximum_fusion.6.k_ref, bf16[128,768]{1,0:T(8,128)(2,1)S(1)} %fusion.72.v_ref), custom_call_target="tpu_custom_call" | custom-call | tf_op jit(solution)/shard_map/attend/pallas_call | solution.py:471
  161.2 3.0 multiply_convert_fusion.7
  166.1 3.0 multiply_convert_fusion.6
  169.1 2.3 multiply_convert_fusion.5
  171.4 3.1 multiply_convert_fusion.4
  184.8 26.3 %attend.3 = (bf16[128,768]{1,0:T(8,128)(2,1)S(1)}, bf16[3,2048,64]{2,1,0:T(8,128)(2,1)S(1)}, f32[8,256]{1,0:T(8,128)S(1)}) custom-call(bf16[128,768]{1,0:T(8,128)(2,1)S(1)} %fusion.74.q_ref, bf16[128,768]{1,0:T(8,128)(2,1)S(1)} %pad_maximum_fusion.7.k_ref, bf16[128,768]{1,0:T(8,128)(2,1)S(1)} %fusion.75.v_ref), custom_call_target="tpu_custom_call" | custom-call | tf_op jit(solution)/shard_map/attend/pallas_call | solution.py:471
  222.9 2.3 fusion.67
  237.9 31.0 %attend_back.2 = (bf16[128,768]{1,0:T(8,128)(2,1)S(1)}, bf16[128,768]{1,0:T(8,128)(2,1)S(1)}, bf16[128,768]{1,0:T(8,128)(2,1)S(1)}) custom-call(bf16[128,768]{1,0:T(8,128)(2,1)S(1)} %pad_maximum_fusion.8.grad_ref, bf16[3,2048,64]{2,1,0:T(8,128)(2,1)S(1)} %get-tuple-element.47.heads_ref, f32[8,256]{1,0:T(8,128)S(1)} %get-tuple-element.48.total_ref), custom_call_target="tpu_custom_call" | custom-call | tf_op jit(solution)/shard_map/attend_back/pallas_call | solution.py:542
  274.4 2.4 convert_reduce_fusion.13
  278.7 2.4 convert_reduce_fusion.12
  281.2 2.5 convert_reduce_fusion.11
  283.6 2.4 convert_reduce_fusion.10
  292.6 27.6 %attend_back.3 = (bf16[128,768]{1,0:T(8,128)(2,1)S(1)}, bf16[128,768]{1,0:T(8,128)(2,1)S(1)}, bf16[128,768]{1,0:T(8,128)(2,1)S(1)}) custom-call(bf16[128,768]{1,0:T(8,128)(2,1)S(1)} %pad_maximum_fusion.11.grad_ref, bf16[3,2048,64]{2,1,0:T(8,128)(2,1)S(1)} %get-tuple-element.52.heads_ref, f32[8,256]{1,0:T(8,128)S(1)} %get-tuple-element.53.total_ref), custom_call_target="tpu_custom_call" | custom-call | tf_op jit(solution)/shard_map/attend_back/pallas_call | solution.py:542
  339.5 3.1 collective-permute-start.5
  352.3 132.8 %all-reduce.2.cloned.1.call-done = f32[2,9216]{1,0:T(2,128)} async-done(((f32[2,9216]{1,0:T(2,128)}), f32[2,9216]{1,0:T(2,128)}) %all-reduce.2.cloned.1.call-update) | async-done | bytes 73744 | tf_op jit(solution)/shard_map/psum | solution.py:804
  491.1 31.6 %move_blocks.3 = bf16[32,96,128]{2,1,0:T(8,128)(2,1)} custom-call(s32[32]{0:T(128)} %order_ref.1, bf16[32,96,128]{2,1,0:T(8,128)(2,1)} %reshape.456.x_ref), custom_call_target="tpu_custom_call" | custom-call | tf_op jit(solution)/shard_map/move_blocks/pallas_call | solution.py:608
  531.7 7.9 %weight_deltas.1 = bf16[3,4,768,768]{3,2,1,0:T(8,128)(2,1)S(1)} custom-call(bf16[2,4,256,768]{3,2,1,0:T(8,128)(2,1)S(1)} %pad_maximum_fusion.1.left_a.left_b, bf16[2,4,256,768]{3,2,1,0:T(8,128)(2,1)S(1)} %pad_maximum_fusion.1.left_a.left_b, bf16[2,3,2,256,768]{4,3,2,1,0:T(8,128)(2,1)S(1)} %pad_maximum_fusion.right_ref), custom_call_target="tpu_custom_call" | custom-call | tf_op jit(solution)/shard_map/weight_deltas/pallas_call | solution.py:637
  539.6 5.0 copy-done
  544.6 68.6 %reduce_grads.1 = f32[3,48,768]{2,1,0:T(8,128)} custom-call(bf16[3,4,4,4,48,768]{5,4,3,2,1,0:T(8,128)(2,1)} %bitcast.384), custom_call_target="tpu_custom_call" | custom-call | tf_op jit(solution)/shard_map/reduce_grads/pallas_call | solution.py:277
  614.3 3.8 collective-permute-start.8
  (313 shorter events, 125.3 us)
Async XLA Ops:
  7.2 477.9 %all-reduce.2.cloned.1.call-start = ((), (), s32[]{:S(2)}) async-start(), calls=%async_computation | async-start | bytes 147456 | tf_op jit(solution)/shard_map/psum | solution.py:804
  13.6 38.6 %collective-permute-start = (f32[9216]{0:T(1024)S(1)}, f32[9216]{0:T(1024)S(1)}, u32[]{:S(2)}, u32[]{:S(2)}) collective-permute-start(f32[9216]{0:T(1024)S(1)} %constant_dynamic-update-slice_fusion), channel_id=1, source_target_pairs={{0,1},{1,0},{2,3},{3,2},{4,5},{5,4},{6,7},{7,6},{8,9},{9,8},{10,11... | collective-permute-start | bytes 110600 | tf_op jit(solution)/shard_map/ppermute | solution.py:666
  20.4 35.5 %collective-permute-start.2 = (bf16[3,24,768]{2,1,0:T(8,128)(2,1)S(1)}, bf16[3,24,768]{2,1,0:T(8,128)(2,1)S(1)}, u32[]{:S(2)}, u32[]{:S(2)}) collective-permute-start(bf16[3,24,768]{2,1,0:T(8,128)(2,1)S(1)} %get-tuple-element.171), channel_id=1, source_target_pairs={{0,2},{2,0},{1,3},{3,1},{4,6},{6,4},{5,7},{7,5},{8,10},{10,8},{9,1... | collective-permute-start | bytes 331784 | tf_op jit(solution)/shard_map/ppermute | solution.py:666
  52.2 2.9 collective-permute-start.1
  53.0 2.1 copy-start.21
  53.0 268.9 %copy-start.19 = (f32[128]{0:T(128)}, f32[128]{0:T(128)S(1)}, u32[]{:S(2)}) copy-start(f32[128]{0:T(128)S(1)} %rsqrt.48) | copy-start | bytes 1540
  134.0 2.2 copy-start.2
  181.9 1.9 copy-start.3
  225.2 3.7 copy-start.13
  225.2 3.7 copy-start.15
  276.9 1.9 copy-start.24
  281.2 2.5 copy-start.23
  325.9 2.0 copy-start.14
  325.9 2.0 copy-start.16
  330.7 2.6 copy-start.20
  333.3 1.9 copy-start.22
  338.3 149.6 %collective-permute-start.3 = (bf16[2,128,768]{2,1,0:T(8,128)(2,1)}, bf16[2,128,768]{2,1,0:T(8,128)(2,1)}, u32[]{:S(2)}, u32[]{:S(2)}) collective-permute-start(bf16[2,128,768]{2,1,0:T(8,128)(2,1)} %maximum_select_fusion.3), channel_id=1, source_target_pairs={{0,64},{64,0},{1,65},{65,1},{2,66},{66,2},{3,67},{67,3},{4,68},{68... | collective-permute-start | bytes 1179656 | tf_op jit(solution)/shard_map/ppermute | solution.py:666
  339.5 185.6 %collective-permute-start.5 = (bf16[4,128,768]{2,1,0:T(8,128)(2,1)}, bf16[4,128,768]{2,1,0:T(8,128)(2,1)}, u32[]{:S(2)}, u32[]{:S(2)}) collective-permute-start(bf16[4,128,768]{2,1,0:T(8,128)(2,1)} %pad_maximum_fusion.5), channel_id=1, source_target_pairs={{0,2},{2,0},{1,3},{3,1},{4,6},{6,4},{5,7},{7,5},{8,10},{10,8},{9,1... | collective-permute-start | bytes 2359304 | tf_op jit(solution)/shard_map/ppermute | solution.py:666
  343.6 183.1 %collective-permute-start.4 = (bf16[4,128,768]{2,1,0:T(8,128)(2,1)}, bf16[4,128,768]{2,1,0:T(8,128)(2,1)}, u32[]{:S(2)}, u32[]{:S(2)}) collective-permute-start(bf16[4,128,768]{2,1,0:T(8,128)(2,1)} %pad_maximum_fusion.4), channel_id=1, source_target_pairs={{0,2},{2,0},{1,3},{3,1},{4,6},{6,4},{5,7},{7,5},{8,10},{10,8},{9,1... | collective-permute-start | bytes 2359304 | tf_op jit(solution)/shard_map/ppermute | solution.py:666
  344.8 183.5 %collective-permute-start.7 = (bf16[3,2,128,768]{3,2,1,0:T(8,128)(2,1)}, bf16[3,2,128,768]{3,2,1,0:T(8,128)(2,1)}, u32[]{:S(2)}, u32[]{:S(2)}) collective-permute-start(bf16[3,2,128,768]{3,2,1,0:T(8,128)(2,1)} %pad_maximum_fusion.3), channel_id=1, source_target_pairs={{0,2},{2,0},{1,3},{3,1},{4,6},{6,4},{5,7},{7,5},{8,10},{10,8},{9,1... | collective-permute-start | bytes 3538952 | tf_op jit(solution)/shard_map/ppermute | solution.py:666
  348.1 181.7 %collective-permute-start.6 = (bf16[3,2,128,768]{3,2,1,0:T(8,128)(2,1)}, bf16[3,2,128,768]{3,2,1,0:T(8,128)(2,1)}, u32[]{:S(2)}, u32[]{:S(2)}) collective-permute-start(bf16[3,2,128,768]{3,2,1,0:T(8,128)(2,1)} %pad_maximum_fusion.2), channel_id=1, source_target_pairs={{0,2},{2,0},{1,3},{3,1},{4,6},{6,4},{5,7},{7,5},{8,10},{10,8},{9,1... | collective-permute-start | bytes 3538952 | tf_op jit(solution)/shard_map/ppermute | solution.py:666
  525.1 1.7 copy-start.12
  539.6 5.1 copy-start
  614.3 4.9 collective-permute-start.8
  (14 other events, 17.8 us)
Sparse Core Ops, SparseCore 0:
  349.5 135.4 all-reduce.1
